TPU v7x, 128 devices: a whole 4x4x4 slice. The times are simulated.
128 devices in a mesh: energy: 64 (over x, z, y), space: 2 (over core).
Axes of the slice: x: 4, y: 4, z: 4, core: 2. Of those that a mesh axis runs over, the one named last changes fastest.
Arguments:
- gr_diag: float32 [1024, 2, 2, 128, 128], P('energy', None, 'space'), may hold values from -1.5 to 1.5
- gr_upper: float32 [1024, 2, 2, 128, 128], P('energy', None, 'space'), may hold values from -1.5 to 1.5
- sigma_lesser: float32 [1024, 2, 2, 128, 128], P('energy', None, 'space'), may hold values from -0.18 to 0.18
- retained: int32 [2, 128, 128], P('space'), may hold values from 0 to 1, as said below
- coulomb: float32 [2, 128, 128], P('space'), may hold values from -0.5 to 0.5
Outputs:
- screened: float32 [1024, 2, 2, 128, 128], P('energy', None, 'space')
Inputs may be any that keep to these rules, and one draw needn't show every extreme that they name: `retained`: entries are 0 or 1; every orbital row of every block row retains exactly 64 elements (value 1).
All inputs are finite; a program needn't handle non-finite values.
Results may differ from a plain program's by a relative error of at most 0.0003.
Values sent between devices are 32-bit elements; how exact they have to be, the bound alone decides.
A program may use at most 192 MiB of HBM per device.

v0:
```python
import functools
import math

import jax
import jax.numpy as jnp
import numpy as np
from jax import lax
from jax.experimental import pallas as pl
from jax.experimental.pallas import tpu as pltpu
from jax.sharding import PartitionSpec as P

MESH = pl.DeviceIdType.MESH
F32 = jnp.float32
BF16 = jnp.bfloat16

SLABS = 8
RADIX = 16
INNER = 128
CHUNKS = 2
ROWS = 8
LENGTH = RADIX * INNER


def transform_tables():
    place = np.arange(INNER)
    chunk, group, row = place // 64, (place // 8) % 8, place % 8
    n2 = 16 * group + 8 * chunk + row
    k1 = np.arange(RADIX)[:, None, None]
    k2 = np.arange(INNER)[None, :, None]
    angle = 2.0 * math.pi / LENGTH * ((n2[None, None, :] * (k1 + RADIX * k2)) % LENGTH)
    cos, sin = np.cos(angle), np.sin(angle)
    ahead = np.concatenate(
        [np.concatenate([cos, sin], axis=2), np.concatenate([-sin, cos], axis=2)], axis=1
    )
    scale = 1.0 / (LENGTH * math.sqrt(SLABS * INNER))
    back = np.swapaxes(ahead, 1, 2) * scale

    def cut(table):
        table = table.astype(np.float32)
        high = table.astype(jnp.bfloat16)
        low = (table - high.astype(np.float32)).astype(jnp.bfloat16)
        return np.stack([high, low])

    return np.stack([cut(ahead), cut(back)])


def cut(value):
    high = value.astype(BF16)
    return high, (value - high.astype(F32)).astype(BF16)


def product(left, right, transposed=False):
    dims = (((1,), (1 if transposed else 0,)), ((), ()))
    dot = functools.partial(lax.dot_general, dimension_numbers=dims, preferred_element_type=F32)
    return dot(left[0], right[0]) + dot(left[1], right[0]) + dot(left[0], right[1])


def each(fn, *pairs):
    return tuple(fn(*parts) for parts in zip(*pairs))


def beside(*parts):
    return jnp.concatenate(parts, axis=1)


def above(*parts):
    return jnp.concatenate(parts, axis=0)


def lesser_greater(gr, gi, sr, si, ur, ui, vr, vi, tr, ti):
    own_g = [cut(gr), cut(gi)]
    own_s = [cut(sr), cut(si)]
    own_u = [cut(ur), cut(ui)]
    far_u = [cut(vr), cut(vi)]
    far_s = [cut(tr), cut(ti)]
    turned_u = [cut(jnp.transpose(vr)), cut(jnp.transpose(vi))]

    def whole(pair):
        return each(lambda r, i: above(beside(r, i), beside(-i, r)), *pair)

    def conjugate(pair):
        return each(lambda r, i: above(beside(r, -i), beside(i, r)), *pair)

    first = product(each(beside, *own_g), whole(own_s))
    both = product(each(lambda a, b, c, d: above(beside(a, b), beside(c, d)), *own_u, *turned_u), whole(far_s))
    total = product(cut(first), whole(own_g), True)
    total = total + product(cut(both[:128]), whole(own_u), True)
    total = total + product(cut(both[128:]), conjugate(far_u))
    lr, li = total[:, :128], total[:, 128:]
    return lr, li, lr + (gr - jnp.transpose(gr)), li + (gi + jnp.transpose(gi))


def take(value, index):
    return jnp.take_along_axis(value, index, axis=1, mode="promise_in_bounds")


def lanes(shape):
    return lax.broadcasted_iota(jnp.int32, shape, 1)


def counts(mask):
    total = mask
    lane = lanes(mask.shape)
    for step in (1, 2, 4, 8, 16, 32, 64):
        total = total + jnp.where(lane >= step, pltpu.roll(total, step, 1), 0)
    return total


def columns_of(count):
    wanted = lanes(count.shape) % 64
    place = jnp.zeros_like(count)
    for step in (64, 32, 16, 8, 4, 2, 1):
        probe = take(count, place + (step - 1))
        place = place + jnp.where(probe <= wanted, step, 0)
    return place


def packed(value, low_index, high_index):
    low = take(value[:64], low_index)
    high = take(value[64:], high_index)
    return jnp.where(lanes(low.shape) < 64, low, high)


def unpacked(value, low_rank, high_rank, mask):
    return above(take(value, low_rank), take(value, high_rank)) * mask


def add(a, b):
    return (a[0] + b[0], a[1] + b[1])


def sub(a, b):
    return (a[0] - b[0], a[1] - b[1])


def turn(a, k, sign):
    k = k % 16
    if k >= 8:
        r, i = turn(a, k - 8, sign)
        return (-r, -i)
    if k == 0:
        return a
    if k == 4:
        return (-a[1], a[0]) if sign > 0 else (a[1], -a[0])
    c, s = math.cos(2 * math.pi * k / 16), sign * math.sin(2 * math.pi * k / 16)
    if k == 2:
        return (c * (a[0] - a[1]), c * (a[0] + a[1])) if sign > 0 else (c * (a[0] + a[1]), c * (a[1] - a[0]))
    if k == 6:
        h = -c
        return (-h * (a[0] + a[1]), h * (a[0] - a[1])) if sign > 0 else (h * (a[1] - a[0]), -h * (a[0] + a[1]))
    return (c * a[0] - s * a[1], s * a[0] + c * a[1])


def dft(values, sign):
    n = len(values)
    if n == 1:
        return values
    even, odd = dft(values[0::2], sign), dft(values[1::2], sign)
    odd = [turn(v, k * (16 // n), sign) for k, v in enumerate(odd)]
    return [add(a, b) for a, b in zip(even, odd)] + [sub(a, b) for a, b in zip(even, odd)]


def split_sixteen(values):
    even = dft(values, -1)
    odd = dft([turn(v, k, -1) for k, v in enumerate(values)], -1)
    return [v for pair in zip(even, odd) for v in pair]


def join_sixteen(values):
    even, odd = dft(values[0::2], 1), dft(values[1::2], 1)
    return [add(a, turn(b, k, 1)) for k, (a, b) in enumerate(zip(even, odd))]


def correlate(recv, table, spread, folded, psend):
    def outer(step, carry):
        chunk, group = step // 8, step % 8
        at = pl.multiple_of(step * 8, 8)
        for which in range(2):
            values = [
                (recv[chunk, n1 * 8 + group, 2 * which], recv[chunk, n1 * 8 + group, 2 * which + 1])
                for n1 in range(SLABS)
            ]
            for k1, (r, i) in enumerate(split_sixteen(values)):
                spread[k1, pl.ds(at, 8), which * 128 : (which + 1) * 128] = r
                spread[k1, pl.ds(at + 128, 8), which * 128 : (which + 1) * 128] = i
        return carry

    lax.fori_loop(0, 16, outer, 0)

    def inner(k1, carry):
        spectrum = product((table[0, 0, k1], table[0, 1, k1]), cut(spread[k1]))
        lr, li = spectrum[:128, :128], spectrum[128:, :128]
        gr, gi = spectrum[:128, 128:], spectrum[128:, 128:]
        cross = above(lr * gr + li * gi, li * gr - lr * gi)
        folded[k1] = product((table[1, 0, k1], table[1, 1, k1]), cut(cross))
        return carry

    lax.fori_loop(0, RADIX, inner, 0, unroll=2)

    def last(step, carry):
        chunk, group = step // 8, step % 8
        at = pl.multiple_of(step * 8, 8)
        values = [(folded[k1, pl.ds(at, 8)], folded[k1, pl.ds(at + 128, 8)]) for k1 in range(RADIX)]
        for n1, (r, i) in enumerate(join_sixteen(values)):
            psend[chunk, n1 * 8 + group, 0] = i
            psend[chunk, n1 * 8 + group, 1] = -r
        return carry

    lax.fori_loop(0, 16, last, 0)


def kernel(
    devices,
    g, u, s, mask, coulomb, tables, out,
    vg, vu, vs, vv, vt, table, send, recv, spread, folded, psend, precv, vout, index, rank,
    load_sem, table_sem, near_send, near_recv, send_sem, recv_sem, back_send, back_recv, out_sem,
):
    me = lax.axis_index("energy")
    side = lax.axis_index("space")
    barrier = pltpu.get_barrier_semaphore()
    pl.semaphore_signal(barrier, inc=1, device_id=(me, 1 - side), device_id_type=MESH)

    def greet(step, carry):
        pl.semaphore_signal(barrier, inc=1, device_id=(lax.rem(me + step, devices), side), device_id_type=MESH)
        return carry

    lax.fori_loop(1, devices, greet, 0)

    loads = []
    for c in range(CHUNKS):
        span = pl.ds(c * ROWS, ROWS)
        for k, (far, near) in enumerate(((g, vg), (s, vs), (u, vu))):
            loads.append(pltpu.make_async_copy(far.at[span], near.at[span], load_sem.at[c, k]))
    for copy in loads:
        copy.start()
    fetch = pltpu.make_async_copy(tables, table, table_sem)
    fetch.start()

    count = counts(mask[...])
    index[0] = columns_of(count[:64])
    index[1] = columns_of(count[64:])
    rank[0] = jnp.maximum(count[:64] - 1, 0)
    rank[1] = jnp.maximum(count[64:] + 63, 0)

    pl.semaphore_wait(barrier, devices)

    exchanges = []
    for c in range(CHUNKS):
        span = pl.ds(c * ROWS, ROWS)
        for k, (far, near) in enumerate(((s, vt), (u, vv))):
            exchanges.append(
                pltpu.make_async_remote_copy(
                    src_ref=far.at[span], dst_ref=near.at[span],
                    send_sem=near_send.at[c, k], recv_sem=near_recv.at[c, k],
                    device_id=(me, 1 - side), device_id_type=MESH,
                )
            )
    for copy in exchanges:
        copy.start()

    for c in range(CHUNKS):
        for k in range(3):
            loads[3 * c + k].wait()
        for k in range(2):
            exchanges[2 * c + k].wait_recv()

        def one_energy(row, carry):
            e = c * ROWS + row
            parts = lesser_greater(
                vg[e, 0], vg[e, 1], vs[e, 0], vs[e, 1], vu[e, 0], vu[e, 1],
                vv[e, 0], vv[e, 1], vt[e, 0], vt[e, 1],
            )
            for k, part in enumerate(parts):
                send[c, pl.ds(k * ROWS + row, devices, stride=4 * ROWS), :] = packed(part, index[0], index[1])
            return carry

        lax.fori_loop(0, ROWS, one_energy, 0)

        block = 4 * ROWS
        mine = pl.ds(pl.multiple_of(me * block, block), block)

        def give(step, carry):
            target = lax.rem(me + step, devices)
            pltpu.make_async_remote_copy(
                src_ref=send.at[c, pl.ds(pl.multiple_of(target * block, block), block)],
                dst_ref=recv.at[c, mine],
                send_sem=send_sem.at[c], recv_sem=recv_sem.at[c],
                device_id=(target, side), device_id_type=MESH,
            ).start()
            return carry

        pltpu.make_async_copy(send.at[c, mine], recv.at[c, mine], recv_sem.at[c]).start()
        lax.fori_loop(1, devices, give, 0)

    fetch.wait()
    for c in range(CHUNKS):
        pltpu.make_async_copy(recv.at[c], recv.at[c], recv_sem.at[c]).wait()

    received = recv.reshape(CHUNKS, devices, 4, ROWS, 128)
    sending = psend.reshape(CHUNKS, devices, 2, ROWS, 128)
    correlate(received, table, spread, folded, sending)

    for c in range(CHUNKS):
        block = 2 * ROWS
        mine = pl.ds(pl.multiple_of(me * block, block), block)

        def give_back(step, carry):
            target = lax.rem(me + step, devices)
            pltpu.make_async_remote_copy(
                src_ref=psend.at[c, pl.ds(pl.multiple_of(target * block, block), block)],
                dst_ref=precv.at[c, mine],
                send_sem=back_send.at[c], recv_sem=back_recv.at[c],
                device_id=(target, side), device_id_type=MESH,
            ).start()
            return carry

        pltpu.make_async_copy(psend.at[c, mine], precv.at[c, mine], back_recv.at[c]).start()
        lax.fori_loop(1, devices, give_back, 0)

    matrix = cut(coulomb[...])
    keep = mask[...].astype(F32)
    outs = []
    for c in range(CHUNKS):
        pltpu.make_async_copy(precv.at[c], precv.at[c], back_recv.at[c]).wait()

        def screen(row, carry):
            e = c * ROWS + row
            parts = [
                unpacked(
                    precv[c, pl.ds(k * ROWS + row, devices, stride=2 * ROWS), :], rank[0], rank[1], keep
                )
                for k in range(2)
            ]
            half = product(cut(above(*parts)), matrix, True)
            full = product(matrix, cut(beside(half[:128], half[128:])))
            vout[e, 0] = full[:, :128]
            vout[e, 1] = full[:, 128:]
            return carry

        lax.fori_loop(0, ROWS, screen, 0, unroll=2)
        span = pl.ds(c * ROWS, ROWS)
        outs.append(pltpu.make_async_copy(vout.at[span], out.at[span], out_sem.at[c]))
        outs[-1].start()

    for copy in exchanges:
        copy.wait_send()
    for c in range(CHUNKS):
        gone = send.at[c, pl.ds(0, (devices - 1) * 4 * ROWS)]
        pltpu.make_async_copy(gone, gone, send_sem.at[c]).wait()
        gone = psend.at[c, pl.ds(0, (devices - 1) * 2 * ROWS)]
        pltpu.make_async_copy(gone, gone, back_send.at[c]).wait()
    for copy in outs:
        copy.wait()


def on_device(devices, gr_diag, gr_upper, sigma_lesser, retained, coulomb):
    shape = gr_diag.shape
    blocks = [array.reshape(16, 2, 128, 128) for array in (gr_diag, gr_upper, sigma_lesser)]
    tables = jnp.asarray(transform_tables())
    block = pltpu.VMEM((16, 2, 128, 128), F32)
    dma = pltpu.SemaphoreType.DMA
    anywhere = pl.BlockSpec(memory_space=pl.ANY)
    near = pl.BlockSpec(memory_space=pltpu.VMEM)
    out = pl.pallas_call(
        functools.partial(kernel, devices),
        out_shape=jax.ShapeDtypeStruct((16, 2, 128, 128), F32),
        in_specs=[anywhere, anywhere, anywhere, near, near, anywhere],
        out_specs=anywhere,
        scratch_shapes=[
            block, block, block, block, block,
            pltpu.VMEM((2, 2, RADIX, 256, 256), BF16),
            pltpu.VMEM((CHUNKS, devices * 4 * ROWS, 128), F32),
            pltpu.VMEM((CHUNKS, devices * 4 * ROWS, 128), F32),
            pltpu.VMEM((RADIX, 256, 256), F32),
            pltpu.VMEM((RADIX, 256, 128), F32),
            pltpu.VMEM((CHUNKS, devices * 2 * ROWS, 128), F32),
            pltpu.VMEM((CHUNKS, devices * 2 * ROWS, 128), F32),
            block,
            pltpu.VMEM((2, 64, 128), jnp.int32),
            pltpu.VMEM((2, 64, 128), jnp.int32),
            dma((CHUNKS, 3)), dma, dma((CHUNKS, 2)), dma((CHUNKS, 2)),
            dma((CHUNKS,)), dma((CHUNKS,)), dma((CHUNKS,)), dma((CHUNKS,)), dma((CHUNKS,)),
        ],
        compiler_params=pltpu.CompilerParams(
            collective_id=0, has_side_effects=True, vmem_limit_bytes=56 * 1024 * 1024
        ),
        cost_estimate=pl.CostEstimate(flops=10**10, bytes_accessed=2 * 10**7, transcendentals=0),
    )(*blocks, retained.reshape(128, 128), coulomb.reshape(128, 128), tables)
    return out.reshape(shape)


def solution(mesh):
    whole = P("energy", None, "space", None, None)
    part = P("space", None, None)
    return jax.shard_map(
        functools.partial(on_device, mesh.shape["energy"]),
        mesh=mesh,
        in_specs=(whole, whole, whole, part, part),
        out_specs=whole,
        check_vma=False,
    )
```

profile of v0, /device:TPU:1, one launch (start us, length us, event | category | flops | bytes accessed | tf_op | source)
XLA Modules:
  0.0 85.2 jit_solution(3644048324119329896)
XLA Ops:
  0.0 82.0 %shard_map.64 = f32[16,2,128,128]{3,2,1,0:T(8,128)} custom-call(f32[16,2,128,128]{3,2,1,0:T(8,128)} %bitcast.9, f32[16,2,128,128]{3,2,1,0:T(8,128)} %bitcast.10, f32[16,2,128,128]{3,2,1,0:T(8,128)} %bitcast.11, s32[128,128]{1,0:T(8,128)} %bitcast.12, f32[128,128]{1,0:T(8,128)} %bitcast.13, bf16[2,2,16,256,256]{4,3,2,1,0:T(8,128)(2,1)} %constant.2.clone.tables), custom_call_target="tpu_custom_call" | custom-call | flops 10000000000 | bytes 20000000 | tf_op jit(solution)/shard_map/pallas_call | solution.py:364
  82.0 3.1 %copy.9 = f32[16,2,1,128,128]{4,3,2,1,0:T(8,128)} copy(f32[16,2,1,128,128]{4,3,2,1,0:T(8,128)} %bitcast.8) | data formatting | bytes 4194304
where the time goes:
time: 86.3 us; the launch traced here: 85.2 us
  Pallas kernels  82 us (95%)
  local copies, waits for them, and re-layouts  3.14 us (4%)
    pallas_call x1, Pallas kernels, on_device(): pl.pallas_call(functools.partial(kernel, devices), out_shape=jax.ShapeDty...  82 us
    unnamed x1, local copies, waits for them, and re-layouts  3.14 us

commit v1 on v0

v1 whole, which is shorter than its diff:
```python
import functools
import math

import jax
import jax.numpy as jnp
import numpy as np
from jax import lax
from jax.experimental import pallas as pl
from jax.experimental.pallas import tpu as pltpu
from jax.sharding import PartitionSpec as P

MESH = pl.DeviceIdType.MESH
F32 = jnp.float32
BF16 = jnp.bfloat16

SLABS = 8
RADIX = 16
INNER = 128
LENGTH = RADIX * INNER
PIECES = 4
PIECE = 4
CHUNKS = 2
ROWS = 8


def high_low(table):
    table = table.astype(np.float32)
    high = table.astype(jnp.bfloat16)
    return high, (table - high.astype(np.float32)).astype(jnp.bfloat16)


def angles(n2):
    k1 = np.arange(RADIX)[:, None, None]
    k2 = np.arange(INNER)[None, :, None]
    return 2.0 * math.pi / LENGTH * ((n2[None, None, :] * (k1 + RADIX * k2)) % LENGTH)


def ahead_tables():
    tables = []
    for piece in range(PIECES):
        pair, place = np.arange(32) // 8, np.arange(32) % 8
        angle = angles(16 * (2 * pair + place // PIECE) + PIECE * piece + place % PIECE)
        cos, sin = np.cos(angle), np.sin(angle)
        real = np.concatenate([cos, sin], axis=2)
        imag = np.concatenate([-sin, cos], axis=2)
        high, low = high_low(np.concatenate([real, imag], axis=1))
        tables.append(np.concatenate([high, low, high], axis=2))
    return np.stack(tables)


def back_tables():
    scale = 1.0 / (LENGTH * math.sqrt(SLABS * INNER))
    tables = []
    for chunk in range(CHUNKS):
        group, row = np.arange(64) // 8, np.arange(64) % 8
        angle = np.swapaxes(angles(16 * group + ROWS * chunk + row), 1, 2)
        cos, sin = np.cos(angle) * scale, np.sin(angle) * scale
        real = np.concatenate([cos, -sin], axis=2)
        imag = np.concatenate([sin, cos], axis=2)
        tables.append(np.concatenate([real, imag], axis=1))
    return np.stack(high_low(np.stack(tables)))


def cut(value):
    high = value.astype(BF16)
    return high, (value - high.astype(F32)).astype(BF16)


def product(left, right, transposed=False):
    dims = (((1,), (1 if transposed else 0,)), ((), ()))
    dot = functools.partial(lax.dot_general, dimension_numbers=dims, preferred_element_type=F32)
    return dot(left[0], right[0]) + dot(left[1], right[0]) + dot(left[0], right[1])


def each(fn, *pairs):
    return tuple(fn(*parts) for parts in zip(*pairs))


def beside(*parts):
    return jnp.concatenate(parts, axis=1)


def above(*parts):
    return jnp.concatenate(parts, axis=0)


def whole(pair):
    return each(lambda r, i: above(beside(r, i), beside(-i, r)), *pair)


def conjugate(pair):
    return each(lambda r, i: above(beside(r, -i), beside(i, r)), *pair)


def lesser_greater(energies):
    held = []
    for g, s, u, v, t in energies:
        turned = [cut(jnp.transpose(part)) for part in v]
        g, s, u, v, t = ([cut(part) for part in pair] for pair in (g, s, u, v, t))
        first = product(each(beside, *g), whole(s))
        rows = each(lambda a, b, c, d: above(beside(a, b), beside(c, d)), *u, *turned)
        both = product(rows, whole(t))
        held.append((g, u, v, cut(first), cut(both[:128]), cut(both[128:])))
    results = []
    for g, u, v, first, second, third in held:
        total = product(first, whole(g), True) + product(second, whole(u), True)
        results.append(total + product(third, conjugate(v)))
    outputs = []
    for (g, *_), total in zip(energies, results):
        lr, li = total[:, :128], total[:, 128:]
        outputs.append((lr, li, lr + (g[0] - jnp.transpose(g[0])), li + (g[1] + jnp.transpose(g[1]))))
    return outputs


def take(value, index):
    return jnp.take_along_axis(value, index, axis=1, mode="promise_in_bounds")


def lanes(shape):
    return lax.broadcasted_iota(jnp.int32, shape, 1)


def counts(mask):
    total = mask
    lane = lanes(mask.shape)
    for step in (1, 2, 4, 8, 16, 32, 64):
        total = total + jnp.where(lane >= step, pltpu.roll(total, step, 1), 0)
    return total


def columns_of(count):
    wanted = lanes(count.shape) % 64
    place = jnp.zeros_like(count)
    for step in (64, 32, 16, 8, 4, 2, 1):
        probe = take(count, place + (step - 1))
        place = place + jnp.where(probe <= wanted, step, 0)
    return place


def packed(value, low_index, high_index):
    low = take(value[:64], low_index)
    high = take(value[64:], high_index)
    return jnp.where(lanes(low.shape) < 64, low, high)


def unpacked(value, low_rank, high_rank, mask):
    return above(take(value, low_rank), take(value, high_rank)) * mask


def add(a, b):
    return (a[0] + b[0], a[1] + b[1])


def sub(a, b):
    return (a[0] - b[0], a[1] - b[1])


def turn(a, k, sign):
    k = k % 16
    if k >= 8:
        r, i = turn(a, k - 8, sign)
        return (-r, -i)
    if k == 0:
        return a
    if k == 4:
        return (-a[1], a[0]) if sign > 0 else (a[1], -a[0])
    c, s = math.cos(2 * math.pi * k / 16), sign * math.sin(2 * math.pi * k / 16)
    if k == 2:
        return (c * (a[0] - a[1]), c * (a[0] + a[1])) if sign > 0 else (c * (a[0] + a[1]), c * (a[1] - a[0]))
    if k == 6:
        h = -c
        return (-h * (a[0] + a[1]), h * (a[0] - a[1])) if sign > 0 else (h * (a[1] - a[0]), -h * (a[0] + a[1]))
    return (c * a[0] - s * a[1], s * a[0] + c * a[1])


def dft(values, sign):
    n = len(values)
    if n == 1:
        return values
    even, odd = dft(values[0::2], sign), dft(values[1::2], sign)
    odd = [turn(v, k * (16 // n), sign) for k, v in enumerate(odd)]
    return [add(a, b) for a, b in zip(even, odd)] + [sub(a, b) for a, b in zip(even, odd)]


def split_sixteen(values):
    even = dft(values, -1)
    odd = dft([turn(v, k, -1) for k, v in enumerate(values)], -1)
    return [v for pair in zip(even, odd) for v in pair]


def join_sixteen(values):
    even, odd = dft(values[0::2], 1), dft(values[1::2], 1)
    return [add(a, turn(b, k, 1)) for k, (a, b) in enumerate(zip(even, odd))]


def forward(piece, recv, table, spread, spectrum):
    def outer(pair, carry):
        at = pl.multiple_of(pair * 8, 8)
        for which in range(2):
            values = []
            for n1 in range(SLABS):
                start = n1 * 8 * 16 + pair * 32 + 2 * which
                values.append(tuple(recv[piece, pl.ds(start + part, 8, stride=4), :] for part in range(2)))
            for k1, (r, i) in enumerate(split_sixteen(values)):
                spread[k1, pl.ds(at, 8), which * 128 : (which + 1) * 128] = r
                spread[k1, pl.ds(at + 32, 8), which * 128 : (which + 1) * 128] = i
        return carry

    lax.fori_loop(0, 4, outer, 0)

    def inner(step, carry):
        for k1 in [step * 4 + k for k in range(4)]:
            high, low = cut(spread[k1])
            spectrum[k1] += jnp.dot(table[piece, k1], above(high, high, low), preferred_element_type=F32)
        return carry

    lax.fori_loop(0, RADIX // 4, inner, 0)


def multiply(spectrum, cross):
    def one(k1, carry):
        lr, li = spectrum[k1, :128, :128], spectrum[k1, 128:, :128]
        gr, gi = spectrum[k1, :128, 128:], spectrum[k1, 128:, 128:]
        high, low = cut(above(lr * gr + li * gi, li * gr - lr * gi))
        cross[k1, :, :128] = high
        cross[k1, :, 128:] = low
        return carry

    lax.fori_loop(0, RADIX, one, 0, unroll=2)


def backward(chunk, table, cross, folded, psend):
    def inner(step, carry):
        for k1 in [step * 8 + k for k in range(8)]:
            both = jnp.dot(table[0, chunk, k1], cross[k1], preferred_element_type=F32)
            low = jnp.dot(table[1, chunk, k1], cross[k1, :, :128], preferred_element_type=F32)
            folded[k1] = both[:, :128] + both[:, 128:] + low
        return carry

    lax.fori_loop(0, RADIX // 8, inner, 0)

    def last(group, carry):
        at = pl.multiple_of(group * 8, 8)
        values = [(folded[k1, pl.ds(at, 8)], folded[k1, pl.ds(at + 64, 8)]) for k1 in range(RADIX)]
        for n1, (r, i) in enumerate(join_sixteen(values)):
            place = pl.multiple_of((n1 * 8 + group) * 2 * ROWS, 8)
            psend[chunk, pl.ds(place, 8), :] = i
            psend[chunk, pl.ds(place + 8, 8), :] = -r
        return carry

    lax.fori_loop(0, 8, last, 0)


def kernel(
    devices,
    g, u, s, mask, coulomb, ahead_hbm, back_hbm, out,
    vg, vu, vs, vv, vt, ahead, back, send, recv, spread, spectrum, cross, folded, psend, precv, index, rank,
    load_sem, table_sem, near_send, near_recv, send_sem, recv_sem, back_send, back_recv,
):
    me = lax.axis_index("energy")
    side = lax.axis_index("space")
    barrier = pltpu.get_barrier_semaphore()
    pl.semaphore_signal(barrier, inc=1, device_id=(me, 1 - side), device_id_type=MESH)

    def greet(step, carry):
        pl.semaphore_signal(barrier, inc=1, device_id=(lax.rem(me + step, devices), side), device_id_type=MESH)
        return carry

    lax.fori_loop(1, devices, greet, 0)

    def load(piece, k):
        span = pl.ds(piece * PIECE, PIECE)
        far, near = ((g, vg), (s, vs), (u, vu))[k]
        return pltpu.make_async_copy(far.at[span], near.at[span], load_sem.at[piece, k])

    def exchange(piece, k):
        span = pl.ds(piece * PIECE, PIECE)
        far, near = ((s, vt), (u, vv))[k]
        return pltpu.make_async_remote_copy(
            src_ref=far.at[span], dst_ref=near.at[span],
            send_sem=near_send.at[piece, k], recv_sem=near_recv.at[piece, k],
            device_id=(me, 1 - side), device_id_type=MESH,
        )

    for piece in range(PIECES):
        for k in range(3):
            load(piece, k).start()
    fetches = [
        pltpu.make_async_copy(ahead_hbm, ahead, table_sem.at[0]),
        pltpu.make_async_copy(back_hbm, back, table_sem.at[1]),
    ]

    count = counts(mask[...])
    index[0] = columns_of(count[:64])
    index[1] = columns_of(count[64:])
    rank[0] = jnp.maximum(count[:64] - 1, 0)
    rank[1] = jnp.maximum(count[64:] + 63, 0)

    pl.semaphore_wait(barrier, devices)

    for piece in range(PIECES):
        for k in range(2):
            exchange(piece, k).start()
    for copy in fetches:
        copy.start()
    spectrum[...] = jnp.zeros(spectrum.shape, F32)

    block = 4 * PIECE
    mine = pl.ds(pl.multiple_of(me * block, block), block)

    def one_piece(piece, carry):
        for k in range(3):
            load(piece, k).wait()
        for k in range(2):
            exchange(piece, k).wait_recv()
        places = [piece * PIECE + row for row in range(PIECE)]
        energies = [[(ref[e, 0], ref[e, 1]) for ref in (vg, vs, vu, vv, vt)] for e in places]
        for row, parts in enumerate(lesser_greater(energies)):
            for k, part in enumerate(parts):
                send[piece, pl.ds(row * 4 + k, devices, stride=block), :] = packed(part, index[0], index[1])

        def give(step, carry):
            target = lax.rem(me + step, devices)
            pltpu.make_async_remote_copy(
                src_ref=send.at[piece, pl.ds(pl.multiple_of(target * block, block), block)],
                dst_ref=recv.at[piece, mine],
                send_sem=send_sem.at[piece], recv_sem=recv_sem.at[piece],
                device_id=(target, side), device_id_type=MESH,
            ).start()
            return carry

        lax.fori_loop(1, devices, give, 0)
        pltpu.make_async_copy(send.at[piece, mine], recv.at[piece, mine], recv_sem.at[piece]).start()
        return carry

    lax.fori_loop(0, PIECES, one_piece, 0)

    fetches[0].wait()

    def take_in(piece, carry):
        pltpu.make_async_copy(recv.at[piece], recv.at[piece], recv_sem.at[piece]).wait()
        forward(piece, recv, ahead, spread, spectrum)
        return carry

    lax.fori_loop(0, PIECES, take_in, 0)
    multiply(spectrum, cross)
    fetches[1].wait()

    back_block = 2 * ROWS
    back_mine = pl.ds(pl.multiple_of(me * back_block, back_block), back_block)

    def return_chunk(chunk, carry):
        backward(chunk, back, cross, folded, psend)

        def give_back(step, carry):
            target = lax.rem(me + step, devices)
            pltpu.make_async_remote_copy(
                src_ref=psend.at[chunk, pl.ds(pl.multiple_of(target * back_block, back_block), back_block)],
                dst_ref=precv.at[chunk, back_mine],
                send_sem=back_send.at[chunk], recv_sem=back_recv.at[chunk],
                device_id=(target, side), device_id_type=MESH,
            ).start()
            return carry

        lax.fori_loop(1, devices, give_back, 0)
        pltpu.make_async_copy(psend.at[chunk, back_mine], precv.at[chunk, back_mine], back_recv.at[chunk]).start()
        return carry

    lax.fori_loop(0, CHUNKS, return_chunk, 0)

    matrix = cut(coulomb[...])
    twice = each(lambda m: above(beside(m, jnp.zeros_like(m)), beside(jnp.zeros_like(m), m)), matrix)
    keep = mask[...].astype(F32)

    def screen(chunk, carry):
        pltpu.make_async_copy(precv.at[chunk], precv.at[chunk], back_recv.at[chunk]).wait()
        blocks = []
        for row in range(ROWS):
            parts = [
                precv[chunk, pl.ds(k * ROWS + row, devices, stride=back_block), :] for k in range(2)
            ]
            blocks.append(beside(*[unpacked(part, rank[0], rank[1], keep) for part in parts]))
        half = product(cut(above(*blocks)), twice, True)
        high, low = cut(beside(*[half[128 * row : 128 * (row + 1)] for row in range(ROWS)]))
        full = jnp.dot(beside(*matrix), above(high, high), preferred_element_type=F32)
        full = full + jnp.dot(matrix[0], low, preferred_element_type=F32)
        for row in range(ROWS):
            out[chunk * ROWS + row, 0] = full[:, 256 * row : 256 * row + 128]
            out[chunk * ROWS + row, 1] = full[:, 256 * row + 128 : 256 * row + 256]
        return carry

    lax.fori_loop(0, CHUNKS, screen, 0)

    for piece in range(PIECES):
        for k in range(2):
            exchange(piece, k).wait_send()
        gone = send.at[piece, pl.ds(0, (devices - 1) * block)]
        pltpu.make_async_copy(gone, gone, send_sem.at[piece]).wait()
    for chunk in range(CHUNKS):
        gone = psend.at[chunk, pl.ds(0, (devices - 1) * back_block)]
        pltpu.make_async_copy(gone, gone, back_send.at[chunk]).wait()


def on_device(devices, gr_diag, gr_upper, sigma_lesser, retained, coulomb):
    shape = gr_diag.shape
    blocks = [array.reshape(16, 2, 128, 128) for array in (gr_diag, gr_upper, sigma_lesser)]
    block = pltpu.VMEM((16, 2, 128, 128), F32)
    dma = pltpu.SemaphoreType.DMA
    anywhere = pl.BlockSpec(memory_space=pl.ANY)
    near = pl.BlockSpec(memory_space=pltpu.VMEM)
    out = pl.pallas_call(
        functools.partial(kernel, devices),
        out_shape=pltpu.VMEM((16, 2, 128, 128), F32),
        in_specs=[anywhere, anywhere, anywhere, near, near, anywhere, anywhere],
        out_specs=near,
        scratch_shapes=[
            block, block, block, block, block,
            pltpu.VMEM((PIECES, RADIX, 256, 192), BF16),
            pltpu.VMEM((2, CHUNKS, RADIX, 128, 256), BF16),
            pltpu.VMEM((PIECES, devices * 4 * PIECE, 128), F32),
            pltpu.VMEM((PIECES, devices * 4 * PIECE, 128), F32),
            pltpu.VMEM((RADIX, 64, 256), F32),
            pltpu.VMEM((RADIX, 256, 256), F32),
            pltpu.VMEM((RADIX, 256, 256), BF16),
            pltpu.VMEM((RADIX, 128, 128), F32),
            pltpu.VMEM((CHUNKS, devices * 2 * ROWS, 128), F32),
            pltpu.VMEM((CHUNKS, devices * 2 * ROWS, 128), F32),
            pltpu.VMEM((2, 64, 128), jnp.int32),
            pltpu.VMEM((2, 64, 128), jnp.int32),
            dma((PIECES, 3)), dma((2,)), dma((PIECES, 2)), dma((PIECES, 2)),
            dma((PIECES,)), dma((PIECES,)), dma((CHUNKS,)), dma((CHUNKS,)),
        ],
        compiler_params=pltpu.CompilerParams(
            collective_id=0, has_side_effects=True, vmem_limit_bytes=60 * 1024 * 1024
        ),
        cost_estimate=pl.CostEstimate(flops=10**10, bytes_accessed=2 * 10**7, transcendentals=0),
    )(
        *blocks, retained.reshape(128, 128), coulomb.reshape(128, 128),
        jnp.asarray(ahead_tables()), jnp.asarray(back_tables()),
    )
    return out.reshape(shape)


def solution(mesh):
    whole = P("energy", None, "space", None, None)
    part = P("space", None, None)
    return jax.shard_map(
        functools.partial(on_device, mesh.shape["energy"]),
        mesh=mesh,
        in_specs=(whole, whole, whole, part, part),
        out_specs=whole,
        check_vma=False,
    )
```

time: 86.3 us -> 64 us (0.74)
  Pallas kernels: 82 us -> 62.2 us
  local copies, waits for them, and re-layouts: 3.14 us -> 1.32 us
    pallas_call x1, Pallas kernels: 82 us -> 62.2 us  [on_device(): pl.pallas_call(functools.partial(kernel, devices), out_shape=pltpu.VMEM((...]
    unnamed x1, local copies, waits for them, and re-layouts: 3.14 us -> 1.32 us
where the time goes in v1:
time: 64 us; the launch traced here: 63.5 us
  Pallas kernels  62.2 us (97%)
  local copies, waits for them, and re-layouts  1.32 us (2%)
    pallas_call x1, Pallas kernels, on_device(): pl.pallas_call(functools.partial(kernel, devices), out_shape=pltpu.VMEM((...  62.2 us
    unnamed x1, local copies, waits for them, and re-layouts  1.32 us

profile of v1, /device:TPU:1, one launch (start us, length us, event | category | flops | bytes accessed | tf_op | source)
XLA Modules:
  0.0 63.5 jit_solution(10174120382961594914)
XLA Ops:
  0.0 62.2 %shard_map.73 = f32[16,2,128,128]{3,2,1,0:T(8,128)S(1)} custom-call(f32[16,2,128,128]{3,2,1,0:T(8,128)} %bitcast.9, f32[16,2,128,128]{3,2,1,0:T(8,128)} %bitcast.10, f32[16,2,128,128]{3,2,1,0:T(8,128)} %bitcast.11, s32[128,128]{1,0:T(8,128)} %bitcast.12, f32[128,128]{1,0:T(8,128)} %bitcast.13, bf16[4,16,256,192]{3,2,1,0:T(8,128)(2,1)} %constant.4.clone.ahead_hbm, ...), custom_call_target="tpu_custom_call" | custom-call | flops 10000000000 | bytes 20000000 | tf_op jit(solution)/shard_map/pallas_call | solution.py:411
  62.2 1.3 %copy.10 = f32[16,2,1,128,128]{4,3,2,1,0:T(8,128)} copy(f32[16,2,1,128,128]{4,3,2,1,0:T(8,128)S(1)} %bitcast.8) | data formatting | bytes 4194304

commit v2 on v1

v2 whole, which is shorter than its diff:
```python
import functools
import math

import jax
import jax.numpy as jnp
import numpy as np
from jax import lax
from jax.experimental import pallas as pl
from jax.experimental.pallas import tpu as pltpu
from jax.sharding import PartitionSpec as P

MESH = pl.DeviceIdType.MESH
F32 = jnp.float32
BF16 = jnp.bfloat16

SLABS = 8
RADIX = 16
INNER = 128
LENGTH = RADIX * INNER
PIECES = 4
PIECE = 4
CHUNKS = 2
HALVES = 2
STRIDE = 11
ROWS = 8


def high_low(table):
    table = table.astype(np.float32)
    high = table.astype(jnp.bfloat16)
    return high, (table - high.astype(np.float32)).astype(jnp.bfloat16)


def angles(n2):
    k1 = np.arange(RADIX)[:, None, None]
    k2 = np.arange(INNER)[None, :, None]
    return 2.0 * math.pi / LENGTH * ((n2[None, None, :] * (k1 + RADIX * k2)) % LENGTH)


def ahead_tables():
    tables = []
    for piece in range(PIECES):
        pair, place = np.arange(32) // 8, np.arange(32) % 8
        angle = angles(16 * (2 * pair + place // PIECE) + PIECE * piece + place % PIECE)
        high, low = high_low(np.concatenate([np.cos(angle), np.sin(angle)], axis=2))
        tables.append(np.concatenate([high, low, high], axis=2))
    return np.stack(tables)


def back_tables():
    scale = 1.0 / (LENGTH * math.sqrt(SLABS * INNER))
    tables = []
    for chunk in range(CHUNKS):
        group, row = np.arange(64) // 8, np.arange(64) % 8
        angle = np.swapaxes(angles(16 * group + ROWS * chunk + row), 1, 2)
        tables.append(np.concatenate([np.cos(angle), np.sin(angle)], axis=2) * scale)
    return np.stack(high_low(np.stack(tables)))


def cut(value):
    high = value.astype(BF16)
    return high, (value - high.astype(F32)).astype(BF16)


def product(left, right, transposed=False):
    dims = (((1,), (1 if transposed else 0,)), ((), ()))
    dot = functools.partial(lax.dot_general, dimension_numbers=dims, preferred_element_type=F32)
    return dot(left[0], right[0]) + dot(left[1], right[0]) + dot(left[0], right[1])


def each(fn, *pairs):
    return tuple(fn(*parts) for parts in zip(*pairs))


def beside(*parts):
    return jnp.concatenate(parts, axis=1)


def above(*parts):
    return jnp.concatenate(parts, axis=0)


def whole(pair):
    return each(lambda r, i: above(beside(r, i), beside(-i, r)), *pair)


def conjugate(pair):
    return each(lambda r, i: above(beside(r, -i), beside(i, r)), *pair)


def own_term(energies):
    held = []
    for g, s in energies:
        g, s = ([cut(part) for part in pair] for pair in (g, s))
        held.append((g, cut(product(each(beside, *g), whole(s)))))
    return [product(first, whole(g), True) for g, first in held]


def coupled_terms(energies):
    held = []
    for u, v, t in energies:
        turned = [cut(jnp.transpose(part)) for part in v]
        u, v, t = ([cut(part) for part in pair] for pair in (u, v, t))
        rows = each(lambda a, b, c, d: above(beside(a, b), beside(c, d)), *u, *turned)
        both = product(rows, whole(t))
        held.append((u, v, cut(both[:128]), cut(both[128:])))
    return [product(second, whole(u), True) + product(third, conjugate(v)) for u, v, second, third in held]


def take(value, index):
    return jnp.take_along_axis(value, index, axis=1, mode="promise_in_bounds")


def lanes(shape):
    return lax.broadcasted_iota(jnp.int32, shape, 1)


def counts(mask):
    total = mask
    lane = lanes(mask.shape)
    for step in (1, 2, 4, 8, 16, 32, 64):
        total = total + jnp.where(lane >= step, pltpu.roll(total, step, 1), 0)
    return total


def columns_of(count):
    wanted = lanes(count.shape) % 64
    place = jnp.zeros_like(count)
    for step in (64, 32, 16, 8, 4, 2, 1):
        probe = take(count, place + (step - 1))
        place = place + jnp.where(probe <= wanted, step, 0)
    return place


def packed(lesser, greater, index):
    low, high = take(lesser, index), take(greater, index)
    return jnp.where(lanes(low.shape) < 64, low, high)


def unpacked(value, rank, mask):
    return beside(take(value, rank) * mask, take(value, rank + 64) * mask)


def add(a, b):
    return (a[0] + b[0], a[1] + b[1])


def sub(a, b):
    return (a[0] - b[0], a[1] - b[1])


def turn(a, k, sign):
    k = k % 16
    if k >= 8:
        r, i = turn(a, k - 8, sign)
        return (-r, -i)
    if k == 0:
        return a
    if k == 4:
        return (-a[1], a[0]) if sign > 0 else (a[1], -a[0])
    c, s = math.cos(2 * math.pi * k / 16), sign * math.sin(2 * math.pi * k / 16)
    if k == 2:
        return (c * (a[0] - a[1]), c * (a[0] + a[1])) if sign > 0 else (c * (a[0] + a[1]), c * (a[1] - a[0]))
    if k == 6:
        h = -c
        return (-h * (a[0] + a[1]), h * (a[0] - a[1])) if sign > 0 else (h * (a[1] - a[0]), -h * (a[0] + a[1]))
    return (c * a[0] - s * a[1], s * a[0] + c * a[1])


def dft(values, sign):
    n = len(values)
    if n == 1:
        return values
    even, odd = dft(values[0::2], sign), dft(values[1::2], sign)
    odd = [turn(v, k * (16 // n), sign) for k, v in enumerate(odd)]
    return [add(a, b) for a, b in zip(even, odd)] + [sub(a, b) for a, b in zip(even, odd)]


def split_sixteen(values):
    even = dft(values, -1)
    odd = dft([turn(v, k, -1) for k, v in enumerate(values)], -1)
    return [v for pair in zip(even, odd) for v in pair]


def join_sixteen(values):
    even, odd = dft(values[0::2], 1), dft(values[1::2], 1)
    return [add(a, turn(b, k, 1)) for k, (a, b) in enumerate(zip(even, odd))]


def forward(half, piece, recv, table, spread, spectrum):
    def outer(pair, carry):
        at = pl.multiple_of(pair * 8, 8)
        values = []
        for n1 in range(SLABS):
            start = n1 * 64 + pair * 16
            values.append(tuple(recv[half, piece, pl.ds(start + part, 8, stride=2), :] for part in range(2)))
        for k1, (r, i) in enumerate(split_sixteen(values)):
            spread[k1, pl.ds(at, 8), :] = r
            spread[k1, pl.ds(at + 32, 8), :] = i
        return carry

    lax.fori_loop(0, 4, outer, 0, unroll=2)

    def inner(step, carry):
        for k1 in [step * 8 + k for k in range(8)]:
            high, low = cut(spread[k1])
            high, low = (beside(v, above(v[32:], -v[:32])) for v in (high, low))
            spectrum[k1] += jnp.dot(table[piece, k1], above(high, high, low), preferred_element_type=F32)
        return carry

    lax.fori_loop(0, RADIX // 8, inner, 0)


def multiply(spectrum, cross):
    def one(k1, carry):
        real, imag = spectrum[k1, :, :128], spectrum[k1, :, 128:]
        real_turned, imag_turned = pltpu.roll(real, 64, 1), pltpu.roll(imag, 64, 1)
        same = real * real_turned + imag * imag_turned
        swapped = real * imag_turned - imag * real_turned
        first = lanes(same.shape) < 64
        cross[k1] = beside(*cut(above(jnp.where(first, same, swapped), jnp.where(first, swapped, same))))
        return carry

    lax.fori_loop(0, RADIX, one, 0, unroll=4)


def backward(half, chunk, table, cross, folded, psend):
    def inner(step, carry):
        for k1 in [step * 8 + k for k in range(8)]:
            both = jnp.dot(table[0, chunk, k1], cross[k1], preferred_element_type=F32)
            low = jnp.dot(table[1, chunk, k1], cross[k1, :, :128], preferred_element_type=F32)
            folded[k1] = both[:, :128] + both[:, 128:] + low
        return carry

    lax.fori_loop(0, RADIX // 8, inner, 0)

    def last(pair, carry):
        at = pl.multiple_of(pair * 16, 8)
        values = []
        for k1 in range(RADIX):
            one, two = folded[k1, pl.ds(at, 8)], folded[k1, pl.ds(at + 8, 8)]
            first = lanes(one.shape) < 64
            values.append((jnp.where(first, one, pltpu.roll(two, 64, 1)), jnp.where(first, pltpu.roll(one, 64, 1), two)))
        for n1, (r, i) in enumerate(join_sixteen(values)):
            place = pl.multiple_of((n1 * 8 + pair * 2) * ROWS, 8)
            first = lanes(r.shape) < 64
            psend[half, chunk, pl.ds(place, 8), :] = jnp.where(first, i, -pltpu.roll(r, 64, 1))
            psend[half, chunk, pl.ds(place + 8, 8), :] = jnp.where(first, pltpu.roll(i, 64, 1), -r)
        return carry

    lax.fori_loop(0, 4, last, 0)


def kernel(
    devices,
    g, u, s, mask, coulomb, ahead_hbm, back_hbm, out,
    vg, vu, vs, vv, vt, ahead, back, send, recv, spread, spectrum, cross, folded, psend, precv, half_done, index, rank, keep, own,
    load_sem, table_sem, near_send, near_recv, send_sem, recv_sem, back_send, back_recv, plane_sem, whole_sem,
):
    me = lax.axis_index("energy")
    side = lax.axis_index("space")
    barrier = pltpu.get_barrier_semaphore()
    pl.semaphore_signal(barrier, inc=1, device_id=(me, 1 - side), device_id_type=MESH)

    lines = []
    for stride in (16, 4, 1):
        digit = lax.rem(me // stride, 4)
        lines.append([me + (lax.rem(digit + step, 4) - digit) * stride for step in (1, 2, 3)])
    for line in lines:
        for other in line:
            pl.semaphore_signal(barrier, inc=1, device_id=(other, side), device_id_type=MESH)

    def load(piece, k):
        span = pl.ds(piece * PIECE, PIECE)
        far, near = ((g, vg), (s, vs), (u, vu))[k]
        return pltpu.make_async_copy(far.at[span], near.at[span], load_sem.at[piece, k])

    def exchange(piece, k):
        span = pl.ds(piece * PIECE, PIECE)
        far, near = ((s, vt), (u, vv))[k]
        return pltpu.make_async_remote_copy(
            src_ref=far.at[span], dst_ref=near.at[span],
            send_sem=near_send.at[piece, k], recv_sem=near_recv.at[piece, k],
            device_id=(me, 1 - side), device_id_type=MESH,
        )

    for piece in range(PIECES):
        for k in range(3):
            load(piece, k).start()
    fetches = [
        pltpu.make_async_copy(ahead_hbm, ahead, table_sem.at[0]),
        pltpu.make_async_copy(back_hbm, back, table_sem.at[1]),
    ]

    def local(piece):
        for k in range(2):
            load(piece, k).wait()
        places = [piece * PIECE + row for row in range(PIECE)]
        for row, term in enumerate(own_term([[(ref[e, 0], ref[e, 1]) for ref in (vg, vs)] for e in places])):
            own[row] = term

    pl.semaphore_wait(barrier, 10)

    for piece in range(PIECES):
        for k in range(2):
            exchange(piece, k).start()
    for other in lines[1]:
        pl.semaphore_signal(plane_sem, inc=1, device_id=(other, side), device_id_type=MESH)
    for copy in fetches:
        copy.start()

    count = counts(mask[...])
    for half in range(HALVES):
        rows = slice(64 * half, 64 * (half + 1))
        index[half] = columns_of(count[rows])
        rank[half] = jnp.maximum(count[rows] - 1, 0)
        keep[half] = mask[rows, :].astype(F32)

    pl.semaphore_wait(plane_sem, 3)
    for other in lines[2]:
        pl.semaphore_signal(whole_sem, inc=1, device_id=(other, side), device_id_type=MESH)
    local(0)

    mine = pl.ds(pl.multiple_of(me * 8, 8), 8)

    def spread_out(source, place, send_sems, recv_sems):
        def give(step, carry):
            target = lax.rem(me + step * STRIDE, devices)
            pltpu.make_async_remote_copy(
                src_ref=source.at[pl.ds(pl.multiple_of(target * 8, 8), 8)], dst_ref=place.at[mine],
                send_sem=send_sems, recv_sem=recv_sems, device_id=(target, side), device_id_type=MESH,
            ).start()
            return carry

        lax.fori_loop(1, devices, give, 0)
        pltpu.make_async_copy(source.at[mine], place.at[mine], recv_sems).start()

    def send_piece(half, piece):
        spread_out(send.at[half, piece], recv.at[half, piece], send_sem.at[half, piece], recv_sem.at[half, piece])

    def one_piece(piece, carry):
        load(piece, 2).wait()
        for k in range(2):
            exchange(piece, k).wait_recv()
        places = [piece * PIECE + row for row in range(PIECE)]
        terms = coupled_terms([[(ref[e, 0], ref[e, 1]) for ref in (vu, vv, vt)] for e in places])
        for row, (e, term) in enumerate(zip(places, terms)):
            term = term + own[row]
            lr, li = term[:, :128], term[:, 128:]
            gr, gi = lr + (vg[e, 0] - jnp.transpose(vg[e, 0])), li + (vg[e, 1] + jnp.transpose(vg[e, 1]))
            for half in range(HALVES):
                rows = slice(64 * half, 64 * (half + 1))
                for part, (lesser, greater) in enumerate(((lr, gr), (li, gi))):
                    send[half, piece, pl.ds(row * 2 + part, devices, stride=8), :] = packed(
                        lesser[rows], greater[rows], index[half]
                    )

        @pl.when(piece == 0)
        def _():
            pl.semaphore_wait(whole_sem, 3)

        send_piece(0, piece)

        @pl.when(piece + 1 < PIECES)
        def _():
            local(piece + 1)

        return carry

    lax.fori_loop(0, PIECES, one_piece, 0)
    for copy in fetches:
        copy.wait()

    def one_half(half, carry):
        spectrum[...] = jnp.zeros(spectrum.shape, F32)

        def take_in(piece, carry):
            @pl.when(half == 0)
            def _():
                send_piece(1, piece)

            place = recv.at[half, piece]
            pltpu.make_async_copy(place, place, recv_sem.at[half, piece]).wait()
            forward(half, piece, recv, ahead, spread, spectrum)
            return carry

        lax.fori_loop(0, PIECES, take_in, 0)
        multiply(spectrum, cross)

        def return_chunk(chunk, carry):
            backward(half, chunk, back, cross, folded, psend)
            spread_out(
                psend.at[half, chunk], precv.at[half, chunk], back_send.at[half, chunk], back_recv.at[half, chunk]
            )
            return carry

        lax.fori_loop(0, CHUNKS, return_chunk, 0)
        return carry

    lax.fori_loop(0, HALVES, one_half, 0)

    matrix = cut(coulomb[...])
    twice = each(lambda m: above(beside(m, jnp.zeros_like(m)), beside(jnp.zeros_like(m), m)), matrix)

    def narrow(half, chunk):
        place = precv.at[half, chunk]
        pltpu.make_async_copy(place, place, back_recv.at[half, chunk]).wait()
        blocks = [
            unpacked(precv[half, chunk, pl.ds(row, devices, stride=8), :], rank[half], keep[half])
            for row in range(ROWS)
        ]
        result = product(cut(above(*blocks)), twice, True)
        for row in range(ROWS):
            half_done[chunk * ROWS + row, 64 * half : 64 * (half + 1), :] = result[64 * row : 64 * (row + 1)]

    def first_half(chunk, carry):
        narrow(0, chunk)
        return carry

    lax.fori_loop(0, CHUNKS, first_half, 0)

    def finish(chunk, carry):
        narrow(1, chunk)
        high, low = cut(beside(*[half_done[chunk * ROWS + row] for row in range(ROWS)]))
        full = jnp.dot(beside(*matrix), above(high, high), preferred_element_type=F32)
        full = full + jnp.dot(matrix[0], low, preferred_element_type=F32)
        for row in range(ROWS):
            out[chunk * ROWS + row, 0] = full[:, 256 * row : 256 * row + 128]
            out[chunk * ROWS + row, 1] = full[:, 256 * row + 128 : 256 * row + 256]
        return carry

    lax.fori_loop(0, CHUNKS, finish, 0)

    for piece in range(PIECES):
        for k in range(2):
            exchange(piece, k).wait_send()
    for half in range(HALVES):
        for piece in range(PIECES):
            gone = send.at[half, piece, pl.ds(0, (devices - 1) * 8)]
            pltpu.make_async_copy(gone, gone, send_sem.at[half, piece]).wait()
        for chunk in range(CHUNKS):
            gone = psend.at[half, chunk, pl.ds(0, (devices - 1) * 8)]
            pltpu.make_async_copy(gone, gone, back_send.at[half, chunk]).wait()


def on_device(devices, gr_diag, gr_upper, sigma_lesser, retained, coulomb):
    shape = gr_diag.shape
    blocks = [array.reshape(16, 2, 128, 128) for array in (gr_diag, gr_upper, sigma_lesser)]
    block = pltpu.VMEM((16, 2, 128, 128), F32)
    dma = pltpu.SemaphoreType.DMA
    anywhere = pl.BlockSpec(memory_space=pl.ANY)
    near = pl.BlockSpec(memory_space=pltpu.VMEM)
    out = pl.pallas_call(
        functools.partial(kernel, devices),
        out_shape=pltpu.VMEM((16, 2, 128, 128), F32),
        in_specs=[anywhere, anywhere, anywhere, near, near, anywhere, anywhere],
        out_specs=near,
        scratch_shapes=[
            block, block, block, block, block,
            pltpu.VMEM((PIECES, RADIX, 128, 192), BF16),
            pltpu.VMEM((2, CHUNKS, RADIX, 64, 256), BF16),
            pltpu.VMEM((HALVES, PIECES, devices * 2 * PIECE, 128), F32),
            pltpu.VMEM((HALVES, PIECES, devices * 2 * PIECE, 128), F32),
            pltpu.VMEM((RADIX, 64, 128), F32),
            pltpu.VMEM((RADIX, 128, 256), F32),
            pltpu.VMEM((RADIX, 256, 256), BF16),
            pltpu.VMEM((RADIX, 64, 128), F32),
            pltpu.VMEM((HALVES, CHUNKS, devices * ROWS, 128), F32),
            pltpu.VMEM((HALVES, CHUNKS, devices * ROWS, 128), F32),
            pltpu.VMEM((16, 128, 256), F32),
            pltpu.VMEM((HALVES, 64, 128), jnp.int32),
            pltpu.VMEM((HALVES, 64, 128), jnp.int32),
            pltpu.VMEM((HALVES, 64, 128), F32),
            pltpu.VMEM((PIECE, 128, 256), F32),
            dma((PIECES, 3)), dma((2,)), dma((PIECES, 2)), dma((PIECES, 2)),
            dma((HALVES, PIECES)), dma((HALVES, PIECES)), dma((HALVES, CHUNKS)), dma((HALVES, CHUNKS)),
            pltpu.SemaphoreType.REGULAR, pltpu.SemaphoreType.REGULAR,
        ],
        compiler_params=pltpu.CompilerParams(
            collective_id=0, has_side_effects=True, vmem_limit_bytes=60 * 1024 * 1024
        ),
        cost_estimate=pl.CostEstimate(flops=10**10, bytes_accessed=2 * 10**7, transcendentals=0),
    )(
        *blocks, retained.reshape(128, 128), coulomb.reshape(128, 128),
        jnp.asarray(ahead_tables()), jnp.asarray(back_tables()),
    )
    return out.reshape(shape)


def solution(mesh):
    whole = P("energy", None, "space", None, None)
    part = P("space", None, None)
    return jax.shard_map(
        functools.partial(on_device, mesh.shape["energy"]),
        mesh=mesh,
        in_specs=(whole, whole, whole, part, part),
        out_specs=whole,
        check_vma=False,
    )
```

time: 64 us -> 58.3 us (0.911)
  Pallas kernels: 62.2 us -> 56.4 us
    pallas_call x1, Pallas kernels: 62.2 us -> 56.4 us  [on_device(): pl.pallas_call(functools.partial(kernel, devices), out_shape=pltpu.VMEM((...]
where the time goes in v2:
time: 58.3 us; the launch traced here: 57.8 us
  Pallas kernels  56.4 us (97%)
  local copies, waits for them, and re-layouts  1.32 us (2%)
    pallas_call x1, Pallas kernels, on_device(): pl.pallas_call(functools.partial(kernel, devices), out_shape=pltpu.VMEM((...  56.4 us
    unnamed x1, local copies, waits for them, and re-layouts  1.32 us

profile of v2, /device:TPU:1, one launch (start us, length us, event | category | flops | bytes accessed | tf_op | source)
XLA Modules:
  0.0 57.8 jit_solution(8343377810884526977)
XLA Ops:
  0.0 56.4 %shard_map.73 = f32[16,2,128,128]{3,2,1,0:T(8,128)S(1)} custom-call(f32[16,2,128,128]{3,2,1,0:T(8,128)} %bitcast.9, f32[16,2,128,128]{3,2,1,0:T(8,128)} %bitcast.10, f32[16,2,128,128]{3,2,1,0:T(8,128)} %bitcast.11, s32[128,128]{1,0:T(8,128)} %bitcast.12, f32[128,128]{1,0:T(8,128)} %bitcast.13, bf16[4,16,128,192]{3,2,1,0:T(8,128)(2,1)} %constant.4.clone.ahead_hbm, ...), custom_call_target="tpu_custom_call" | custom-call | flops 10000000000 | bytes 20000000 | tf_op jit(solution)/shard_map/pallas_call | solution.py:453
  56.4 1.3 %copy.10 = f32[16,2,1,128,128]{4,3,2,1,0:T(8,128)} copy(f32[16,2,1,128,128]{4,3,2,1,0:T(8,128)S(1)} %bitcast.8) | data formatting | bytes 4194304

commit v3 on v2

--- a/solution.py
+++ b/solution.py
@@ -21,6 +21,7 @@
 PIECE = 4
 CHUNKS = 2
 HALVES = 2
+BATCH = 8
 STRIDE = 11
 ROWS = 8
 
@@ -49,12 +50,10 @@
 
 def back_tables():
     scale = 1.0 / (LENGTH * math.sqrt(SLABS * INNER))
-    tables = []
-    for chunk in range(CHUNKS):
-        group, row = np.arange(64) // 8, np.arange(64) % 8
-        angle = np.swapaxes(angles(16 * group + ROWS * chunk + row), 1, 2)
-        tables.append(np.concatenate([np.cos(angle), np.sin(angle)], axis=2) * scale)
-    return np.stack(high_low(np.stack(tables)))
+    place = np.arange(INNER)
+    n2 = 16 * (place // 8 % 8) + ROWS * (place // 64) + place % 8
+    angle = np.swapaxes(angles(n2), 1, 2)
+    return np.stack(high_low(np.concatenate([np.cos(angle), np.sin(angle)], axis=2) * scale))
 
 
 def cut(value):
@@ -187,7 +186,7 @@
     return [add(a, turn(b, k, 1)) for k, (a, b) in enumerate(zip(even, odd))]
 
 
-def forward(half, piece, recv, table, spread, spectrum):
+def gather_piece(half, piece, recv, spread):
     def outer(pair, carry):
         at = pl.multiple_of(pair * 8, 8)
         values = []
@@ -201,41 +200,50 @@
 
     lax.fori_loop(0, 4, outer, 0, unroll=2)
 
+
+def partial_spectrum(k1, piece, table, spread):
+    high, low = cut(spread[k1])
+    high, low = (beside(v, above(v[32:], -v[:32])) for v in (high, low))
+    return jnp.dot(table[piece, k1], above(high, high, low), preferred_element_type=F32)
+
+
+def forward(half, piece, recv, table, spread, spectrum):
+    gather_piece(half, piece, recv, spread)
+
     def inner(step, carry):
         for k1 in [step * 8 + k for k in range(8)]:
-            high, low = cut(spread[k1])
-            high, low = (beside(v, above(v[32:], -v[:32])) for v in (high, low))
-            spectrum[k1] += jnp.dot(table[piece, k1], above(high, high, low), preferred_element_type=F32)
+            spectrum[k1] += partial_spectrum(k1, piece, table, spread)
         return carry
 
     lax.fori_loop(0, RADIX // 8, inner, 0)
 
 
-def multiply(spectrum, cross):
-    def one(k1, carry):
-        real, imag = spectrum[k1, :, :128], spectrum[k1, :, 128:]
-        real_turned, imag_turned = pltpu.roll(real, 64, 1), pltpu.roll(imag, 64, 1)
-        same = real * real_turned + imag * imag_turned
-        swapped = real * imag_turned - imag * real_turned
-        first = lanes(same.shape) < 64
-        cross[k1] = beside(*cut(above(jnp.where(first, same, swapped), jnp.where(first, swapped, same))))
-        return carry
-
-    lax.fori_loop(0, RADIX, one, 0, unroll=4)
-
-
-def backward(half, chunk, table, cross, folded, psend):
+def crossed(value):
+    real, imag = value[:, :128], value[:, 128:]
+    real_turned, imag_turned = pltpu.roll(real, 64, 1), pltpu.roll(imag, 64, 1)
+    same = real * real_turned + imag * imag_turned
+    swapped = real * imag_turned - imag * real_turned
+    first = lanes(same.shape) < 64
+    return cut(above(jnp.where(first, same, swapped), jnp.where(first, swapped, same)))
+
+
+def turn_back(half, piece, recv, ahead, back, spread, spectrum, folded):
+    gather_piece(half, piece, recv, spread)
+
     def inner(step, carry):
-        for k1 in [step * 8 + k for k in range(8)]:
-            both = jnp.dot(table[0, chunk, k1], cross[k1], preferred_element_type=F32)
-            low = jnp.dot(table[1, chunk, k1], cross[k1, :, :128], preferred_element_type=F32)
-            folded[k1] = both[:, :128] + both[:, 128:] + low
-        return carry
-
-    lax.fori_loop(0, RADIX // 8, inner, 0)
-
+        places = [step * BATCH + k for k in range(BATCH)]
+        pairs = [crossed(spectrum[k1] + partial_spectrum(k1, piece, ahead, spread)) for k1 in places]
+        for k1, (high, low) in zip(places, pairs):
+            both = jnp.dot(back[0, k1], beside(high, low), preferred_element_type=F32)
+            folded[k1] = both[:, :128] + both[:, 128:] + jnp.dot(back[1, k1], high, preferred_element_type=F32)
+        return carry
+
+    lax.fori_loop(0, RADIX // BATCH, inner, 0)
+
+
+def pack_back(half, chunk, folded, psend):
     def last(pair, carry):
-        at = pl.multiple_of(pair * 16, 8)
+        at = pl.multiple_of(chunk * 64 + pair * 16, 8)
         values = []
         for k1 in range(RADIX):
             one, two = folded[k1, pl.ds(at, 8)], folded[k1, pl.ds(at + 8, 8)]
@@ -248,13 +256,13 @@
             psend[half, chunk, pl.ds(place + 8, 8), :] = jnp.where(first, pltpu.roll(i, 64, 1), -r)
         return carry
 
-    lax.fori_loop(0, 4, last, 0)
+    lax.fori_loop(0, 4, last, 0, unroll=2)
 
 
 def kernel(
     devices,
     g, u, s, mask, coulomb, ahead_hbm, back_hbm, out,
-    vg, vu, vs, vv, vt, ahead, back, send, recv, spread, spectrum, cross, folded, psend, precv, half_done, index, rank, keep, own,
+    vg, vu, vs, vv, vt, ahead, back, send, recv, spread, spectrum, folded, psend, precv, half_done, index, rank, keep, own,
     load_sem, table_sem, near_send, near_recv, send_sem, recv_sem, back_send, back_recv, plane_sem, whole_sem,
 ):
     me = lax.axis_index("energy")
@@ -323,20 +331,30 @@
 
     mine = pl.ds(pl.multiple_of(me * 8, 8), 8)
 
-    def spread_out(source, place, send_sems, recv_sems):
+    def spread_out(source, place, send_to, recv_from):
+        lead = (slice(None),) * (len(source.shape) - 2)
+
         def give(step, carry):
             target = lax.rem(me + step * STRIDE, devices)
             pltpu.make_async_remote_copy(
-                src_ref=source.at[pl.ds(pl.multiple_of(target * 8, 8), 8)], dst_ref=place.at[mine],
-                send_sem=send_sems, recv_sem=recv_sems, device_id=(target, side), device_id_type=MESH,
+                src_ref=source.at[(*lead, pl.ds(pl.multiple_of(target * 8, 8), 8))], dst_ref=place.at[(*lead, mine)],
+                send_sem=send_to, recv_sem=recv_from, device_id=(target, side), device_id_type=MESH,
             ).start()
             return carry
 
-        lax.fori_loop(1, devices, give, 0)
-        pltpu.make_async_copy(source.at[mine], place.at[mine], recv_sems).start()
-
-    def send_piece(half, piece):
-        spread_out(send.at[half, piece], recv.at[half, piece], send_sem.at[half, piece], recv_sem.at[half, piece])
+        lax.fori_loop(1, devices, give, 0, unroll=9)
+        pltpu.make_async_copy(source.at[(*lead, mine)], place.at[(*lead, mine)], recv_from).start()
+
+    def send_first(piece):
+        spread_out(send.at[0, piece], recv.at[0, piece], send_sem.at[0, piece], recv_sem.at[0, piece])
+
+    early, final = pl.ds(0, PIECES - 1), pl.ds(PIECES - 1, 1)
+
+    def send_second(group, k):
+        spread_out(send.at[1, group], recv.at[1, group], send_sem.at[1, k], recv_sem.at[1, k])
+
+    def arrived(place, sem):
+        pltpu.make_async_copy(place, place, sem).wait()
 
     def one_piece(piece, carry):
         load(piece, 2).wait()
@@ -359,7 +377,7 @@
         def _():
             pl.semaphore_wait(whole_sem, 3)
 
-        send_piece(0, piece)
+        send_first(piece)
 
         @pl.when(piece + 1 < PIECES)
         def _():
@@ -371,40 +389,44 @@
     for copy in fetches:
         copy.wait()
 
-    def one_half(half, carry):
-        spectrum[...] = jnp.zeros(spectrum.shape, F32)
-
-        def take_in(piece, carry):
-            @pl.when(half == 0)
-            def _():
-                send_piece(1, piece)
-
-            place = recv.at[half, piece]
-            pltpu.make_async_copy(place, place, recv_sem.at[half, piece]).wait()
-            forward(half, piece, recv, ahead, spread, spectrum)
-            return carry
-
-        lax.fori_loop(0, PIECES, take_in, 0)
-        multiply(spectrum, cross)
-
-        def return_chunk(chunk, carry):
-            backward(half, chunk, back, cross, folded, psend)
-            spread_out(
-                psend.at[half, chunk], precv.at[half, chunk], back_send.at[half, chunk], back_recv.at[half, chunk]
-            )
-            return carry
-
-        lax.fori_loop(0, CHUNKS, return_chunk, 0)
-        return carry
-
-    lax.fori_loop(0, HALVES, one_half, 0)
+    send_second(early, 0)
+    send_second(final, 1)
+
+    spectrum[...] = jnp.zeros(spectrum.shape, F32)
+
+    def take_first(piece, carry):
+        arrived(recv.at[0, piece], recv_sem.at[0, piece])
+        forward(0, piece, recv, ahead, spread, spectrum)
+        return carry
+
+    lax.fori_loop(0, PIECES - 1, take_first, 0)
+    arrived(recv.at[0, PIECES - 1], recv_sem.at[0, PIECES - 1])
+    turn_back(0, PIECES - 1, recv, ahead, back, spread, spectrum, folded)
+    for chunk in range(CHUNKS):
+        pack_back(0, chunk, folded, psend)
+    spread_out(psend.at[0], precv.at[0], back_send.at[0, 0], back_recv.at[0, 0])
+    spectrum[...] = jnp.zeros(spectrum.shape, F32)
+    arrived(recv.at[1, early], recv_sem.at[1, 0])
+
+    def take_second(piece, carry):
+        forward(1, piece, recv, ahead, spread, spectrum)
+        return carry
+
+    lax.fori_loop(0, PIECES - 1, take_second, 0)
+    arrived(recv.at[1, final], recv_sem.at[1, 1])
+    turn_back(1, PIECES - 1, recv, ahead, back, spread, spectrum, folded)
+
+    def return_chunk(chunk, carry):
+        pack_back(1, chunk, folded, psend)
+        spread_out(psend.at[1, chunk], precv.at[1, chunk], back_send.at[1, chunk], back_recv.at[1, chunk])
+        return carry
+
+    lax.fori_loop(0, CHUNKS, return_chunk, 0)
 
     matrix = cut(coulomb[...])
     twice = each(lambda m: above(beside(m, jnp.zeros_like(m)), beside(jnp.zeros_like(m), m)), matrix)
 
     def narrow(half, chunk):
-        place = precv.at[half, chunk]
-        pltpu.make_async_copy(place, place, back_recv.at[half, chunk]).wait()
         blocks = [
             unpacked(precv[half, chunk, pl.ds(row, devices, stride=8), :], rank[half], keep[half])
             for row in range(ROWS)
@@ -413,6 +435,8 @@
         for row in range(ROWS):
             half_done[chunk * ROWS + row, 64 * half : 64 * (half + 1), :] = result[64 * row : 64 * (row + 1)]
 
+    arrived(precv.at[0], back_recv.at[0, 0])
+
     def first_half(chunk, carry):
         narrow(0, chunk)
         return carry
@@ -420,6 +444,7 @@
     lax.fori_loop(0, CHUNKS, first_half, 0)
 
     def finish(chunk, carry):
+        arrived(precv.at[1, chunk], back_recv.at[1, chunk])
         narrow(1, chunk)
         high, low = cut(beside(*[half_done[chunk * ROWS + row] for row in range(ROWS)]))
         full = jnp.dot(beside(*matrix), above(high, high), preferred_element_type=F32)
@@ -434,13 +459,14 @@
     for piece in range(PIECES):
         for k in range(2):
             exchange(piece, k).wait_send()
-    for half in range(HALVES):
-        for piece in range(PIECES):
-            gone = send.at[half, piece, pl.ds(0, (devices - 1) * 8)]
-            pltpu.make_async_copy(gone, gone, send_sem.at[half, piece]).wait()
-        for chunk in range(CHUNKS):
-            gone = psend.at[half, chunk, pl.ds(0, (devices - 1) * 8)]
-            pltpu.make_async_copy(gone, gone, back_send.at[half, chunk]).wait()
+    others = pl.ds(0, (devices - 1) * 8)
+    for piece in range(PIECES):
+        arrived(send.at[0, piece, others], send_sem.at[0, piece])
+    arrived(send.at[1, early, others], send_sem.at[1, 0])
+    arrived(send.at[1, final, others], send_sem.at[1, 1])
+    arrived(psend.at[0, :, others], back_send.at[0, 0])
+    for chunk in range(CHUNKS):
+        arrived(psend.at[1, chunk, others], back_send.at[1, chunk])
 
 
 def on_device(devices, gr_diag, gr_upper, sigma_lesser, retained, coulomb):
@@ -458,13 +484,12 @@
         scratch_shapes=[
             block, block, block, block, block,
             pltpu.VMEM((PIECES, RADIX, 128, 192), BF16),
-            pltpu.VMEM((2, CHUNKS, RADIX, 64, 256), BF16),
+            pltpu.VMEM((2, RADIX, 128, 256), BF16),
             pltpu.VMEM((HALVES, PIECES, devices * 2 * PIECE, 128), F32),
             pltpu.VMEM((HALVES, PIECES, devices * 2 * PIECE, 128), F32),
             pltpu.VMEM((RADIX, 64, 128), F32),
             pltpu.VMEM((RADIX, 128, 256), F32),
-            pltpu.VMEM((RADIX, 256, 256), BF16),
-            pltpu.VMEM((RADIX, 64, 128), F32),
+            pltpu.VMEM((RADIX, 128, 128), F32),
             pltpu.VMEM((HALVES, CHUNKS, devices * ROWS, 128), F32),
             pltpu.VMEM((HALVES, CHUNKS, devices * ROWS, 128), F32),
             pltpu.VMEM((16, 128, 256), F32),

time: 58.3 us -> 55.6 us (0.954)
  Pallas kernels: 56.4 us -> 54 us
    pallas_call x1, Pallas kernels: 56.4 us -> 54 us  [on_device(): pl.pallas_call(functools.partial(kernel, devices), out_shape=pltpu.VMEM((...]
where the time goes in v3:
time: 55.6 us; the launch traced here: 55.4 us
  Pallas kernels  54 us (97%)
  local copies, waits for them, and re-layouts  1.32 us (2%)
    pallas_call x1, Pallas kernels, on_device(): pl.pallas_call(functools.partial(kernel, devices), out_shape=pltpu.VMEM((...  54 us
    unnamed x1, local copies, waits for them, and re-layouts  1.32 us

profile of v3, /device:TPU:1, one launch (start us, length us, event | category | flops | bytes accessed | tf_op | source)
XLA Modules:
  0.0 55.4 jit_solution(1538572496560217278)
XLA Ops:
  0.0 54.0 %shard_map.73 = f32[16,2,128,128]{3,2,1,0:T(8,128)S(1)} custom-call(f32[16,2,128,128]{3,2,1,0:T(8,128)} %bitcast.9, f32[16,2,128,128]{3,2,1,0:T(8,128)} %bitcast.10, f32[16,2,128,128]{3,2,1,0:T(8,128)} %bitcast.11, s32[128,128]{1,0:T(8,128)} %bitcast.12, f32[128,128]{1,0:T(8,128)} %bitcast.13, bf16[4,16,128,192]{3,2,1,0:T(8,128)(2,1)} %constant.4.clone.ahead_hbm, ...), custom_call_target="tpu_custom_call" | custom-call | flops 10000000000 | bytes 20000000 | tf_op jit(solution)/shard_map/pallas_call | solution.py:479
  54.0 1.3 %copy.10 = f32[16,2,1,128,128]{4,3,2,1,0:T(8,128)} copy(f32[16,2,1,128,128]{4,3,2,1,0:T(8,128)S(1)} %bitcast.8) | data formatting | bytes 4194304

commit v4 on v3

--- a/solution.py
+++ b/solution.py
@@ -61,9 +61,8 @@
     return high, (value - high.astype(F32)).astype(BF16)
 
 
-def product(left, right, transposed=False):
-    dims = (((1,), (1 if transposed else 0,)), ((), ()))
-    dot = functools.partial(lax.dot_general, dimension_numbers=dims, preferred_element_type=F32)
+def product(left, right):
+    dot = functools.partial(jnp.dot, preferred_element_type=F32)
     return dot(left[0], right[0]) + dot(left[1], right[0]) + dot(left[0], right[1])
 
 
@@ -90,20 +89,23 @@
 def own_term(energies):
     held = []
     for g, s in energies:
+        turned_g = [cut(jnp.transpose(part)) for part in g]
         g, s = ([cut(part) for part in pair] for pair in (g, s))
-        held.append((g, cut(product(each(beside, *g), whole(s)))))
-    return [product(first, whole(g), True) for g, first in held]
+        held.append((turned_g, cut(product(each(beside, *g), whole(s)))))
+    return [product(first, conjugate(turned_g)) for turned_g, first in held]
 
 
 def coupled_terms(energies):
     held = []
     for u, v, t in energies:
-        turned = [cut(jnp.transpose(part)) for part in v]
+        turned_u, turned_v = ([cut(jnp.transpose(part)) for part in pair] for pair in (u, v))
         u, v, t = ([cut(part) for part in pair] for pair in (u, v, t))
-        rows = each(lambda a, b, c, d: above(beside(a, b), beside(c, d)), *u, *turned)
+        rows = each(lambda a, b, c, d: above(beside(a, b), beside(c, d)), *u, *turned_v)
         both = product(rows, whole(t))
-        held.append((u, v, cut(both[:128]), cut(both[128:])))
-    return [product(second, whole(u), True) + product(third, conjugate(v)) for u, v, second, third in held]
+        held.append((turned_u, v, cut(both[:128]), cut(both[128:])))
+    return [
+        product(second, conjugate(turned_u)) + product(third, conjugate(v)) for turned_u, v, second, third in held
+    ]
 
 
 def take(value, index):
@@ -342,7 +344,7 @@
             ).start()
             return carry
 
-        lax.fori_loop(1, devices, give, 0, unroll=9)
+        lax.fori_loop(1, devices, give, 0, unroll=21)
         pltpu.make_async_copy(source.at[(*lead, mine)], place.at[(*lead, mine)], recv_from).start()
 
     def send_first(piece):
@@ -424,14 +426,15 @@
     lax.fori_loop(0, CHUNKS, return_chunk, 0)
 
     matrix = cut(coulomb[...])
-    twice = each(lambda m: above(beside(m, jnp.zeros_like(m)), beside(jnp.zeros_like(m), m)), matrix)
+    turned_matrix = cut(jnp.transpose(coulomb[...]))
+    twice = each(lambda m: above(beside(m, jnp.zeros_like(m)), beside(jnp.zeros_like(m), m)), turned_matrix)
 
     def narrow(half, chunk):
         blocks = [
             unpacked(precv[half, chunk, pl.ds(row, devices, stride=8), :], rank[half], keep[half])
             for row in range(ROWS)
         ]
-        result = product(cut(above(*blocks)), twice, True)
+        result = product(cut(above(*blocks)), twice)
         for row in range(ROWS):
             half_done[chunk * ROWS + row, 64 * half : 64 * (half + 1), :] = result[64 * row : 64 * (row + 1)]
 

time: 55.6 us -> 55.3 us (level)
  no operation moved by 1% of the time
where the time goes in v4:
time: 55.3 us; the launch traced here: 55.2 us
  Pallas kernels  53.8 us (97%)
  local copies, waits for them, and re-layouts  1.32 us (2%)
    pallas_call x1, Pallas kernels, on_device(): pl.pallas_call(functools.partial(kernel, devices), out_shape=pltpu.VMEM((...  53.8 us
    unnamed x1, local copies, waits for them, and re-layouts  1.32 us

profile of v4, /device:TPU:1, one launch (start us, length us, event | category | flops | bytes accessed | tf_op | source)
XLA Modules:
  0.0 55.2 jit_solution(3528010007748099097)
XLA Ops:
  0.0 53.8 %shard_map.73 = f32[16,2,128,128]{3,2,1,0:T(8,128)S(1)} custom-call(f32[16,2,128,128]{3,2,1,0:T(8,128)} %bitcast.9, f32[16,2,128,128]{3,2,1,0:T(8,128)} %bitcast.10, f32[16,2,128,128]{3,2,1,0:T(8,128)} %bitcast.11, s32[128,128]{1,0:T(8,128)} %bitcast.12, f32[128,128]{1,0:T(8,128)} %bitcast.13, bf16[4,16,128,192]{3,2,1,0:T(8,128)(2,1)} %constant.4.clone.ahead_hbm, ...), custom_call_target="tpu_custom_call" | custom-call | flops 10000000000 | bytes 20000000 | tf_op jit(solution)/shard_map/pallas_call | solution.py:482
  53.8 1.3 %copy.10 = f32[16,2,1,128,128]{4,3,2,1,0:T(8,128)} copy(f32[16,2,1,128,128]{4,3,2,1,0:T(8,128)S(1)} %bitcast.8) | data formatting | bytes 4194304

commit v5 on v4

--- a/solution.py
+++ b/solution.py
@@ -22,7 +22,10 @@
 CHUNKS = 2
 HALVES = 2
 BATCH = 8
-STRIDE = 11
+OFFSETS = sorted(
+    [(k // 16, k // 4 % 4, k % 4) for k in (step * 11 % 64 for step in range(1, 64))],
+    key=lambda steps: -sum(min(step, 4 - step) for step in steps),
+)
 ROWS = 8
 
 
@@ -333,18 +336,19 @@
 
     mine = pl.ds(pl.multiple_of(me * 8, 8), 8)
 
+    at_x, at_z, at_y = (
+        [lax.rem(lax.rem(me // stride, 4) + step, 4) * stride for step in range(4)] for stride in (16, 4, 1)
+    )
+
     def spread_out(source, place, send_to, recv_from):
         lead = (slice(None),) * (len(source.shape) - 2)
 
-        def give(step, carry):
-            target = lax.rem(me + step * STRIDE, devices)
+        for a, b, c in OFFSETS:
+            target = at_x[a] + at_z[b] + at_y[c]
             pltpu.make_async_remote_copy(
                 src_ref=source.at[(*lead, pl.ds(pl.multiple_of(target * 8, 8), 8))], dst_ref=place.at[(*lead, mine)],
                 send_sem=send_to, recv_sem=recv_from, device_id=(target, side), device_id_type=MESH,
             ).start()
-            return carry
-
-        lax.fori_loop(1, devices, give, 0, unroll=21)
         pltpu.make_async_copy(source.at[(*lead, mine)], place.at[(*lead, mine)], recv_from).start()
 
     def send_first(piece):

time: 55.3 us -> 54.3 us (0.982)
  Pallas kernels: 53.8 us -> 52.8 us
    pallas_call x1, Pallas kernels: 53.8 us -> 52.8 us  [on_device(): pl.pallas_call(functools.partial(kernel, devices), out_shape=pltpu.VMEM((...]
where the time goes in v5:
time: 54.3 us; the launch traced here: 54.1 us
  Pallas kernels  52.8 us (97%)
  local copies, waits for them, and re-layouts  1.32 us (2%)
    pallas_call x1, Pallas kernels, on_device(): pl.pallas_call(functools.partial(kernel, devices), out_shape=pltpu.VMEM((...  52.8 us
    unnamed x1, local copies, waits for them, and re-layouts  1.32 us

profile of v5, /device:TPU:1, one launch (start us, length us, event | category | flops | bytes accessed | tf_op | source)
XLA Modules:
  0.0 54.1 jit_solution(14178371046675816896)
XLA Ops:
  0.0 52.8 %shard_map.73 = f32[16,2,128,128]{3,2,1,0:T(8,128)S(1)} custom-call(f32[16,2,128,128]{3,2,1,0:T(8,128)} %bitcast.9, f32[16,2,128,128]{3,2,1,0:T(8,128)} %bitcast.10, f32[16,2,128,128]{3,2,1,0:T(8,128)} %bitcast.11, s32[128,128]{1,0:T(8,128)} %bitcast.12, f32[128,128]{1,0:T(8,128)} %bitcast.13, bf16[4,16,128,192]{3,2,1,0:T(8,128)(2,1)} %constant.4.clone.ahead_hbm, ...), custom_call_target="tpu_custom_call" | custom-call | flops 10000000000 | bytes 20000000 | tf_op jit(solution)/shard_map/pallas_call | solution.py:486
  52.8 1.3 %copy.10 = f32[16,2,1,128,128]{4,3,2,1,0:T(8,128)} copy(f32[16,2,1,128,128]{4,3,2,1,0:T(8,128)S(1)} %bitcast.8) | data formatting | bytes 4194304

commit v6 on v5

--- a/solution.py
+++ b/solution.py
@@ -410,7 +410,7 @@
     turn_back(0, PIECES - 1, recv, ahead, back, spread, spectrum, folded)
     for chunk in range(CHUNKS):
         pack_back(0, chunk, folded, psend)
-    spread_out(psend.at[0], precv.at[0], back_send.at[0, 0], back_recv.at[0, 0])
+        spread_out(psend.at[0, chunk], precv.at[0, chunk], back_send.at[0, chunk], back_recv.at[0, chunk])
     spectrum[...] = jnp.zeros(spectrum.shape, F32)
     arrived(recv.at[1, early], recv_sem.at[1, 0])
 
@@ -442,9 +442,8 @@
         for row in range(ROWS):
             half_done[chunk * ROWS + row, 64 * half : 64 * (half + 1), :] = result[64 * row : 64 * (row + 1)]
 
-    arrived(precv.at[0], back_recv.at[0, 0])
-
     def first_half(chunk, carry):
+        arrived(precv.at[0, chunk], back_recv.at[0, chunk])
         narrow(0, chunk)
         return carry
 
@@ -471,8 +470,8 @@
         arrived(send.at[0, piece, others], send_sem.at[0, piece])
     arrived(send.at[1, early, others], send_sem.at[1, 0])
     arrived(send.at[1, final, others], send_sem.at[1, 1])
-    arrived(psend.at[0, :, others], back_send.at[0, 0])
     for chunk in range(CHUNKS):
+        arrived(psend.at[0, chunk, others], back_send.at[0, chunk])
         arrived(psend.at[1, chunk, others], back_send.at[1, chunk])
 
 

time: 54.3 us -> 53.8 us (level)
  no operation moved by 1% of the time
where the time goes in v6:
time: 53.8 us; the launch traced here: 53.6 us
  Pallas kernels  52.3 us (97%)
  local copies, waits for them, and re-layouts  1.32 us (2%)
    pallas_call x1, Pallas kernels, on_device(): pl.pallas_call(functools.partial(kernel, devices), out_shape=pltpu.VMEM((...  52.3 us
    unnamed x1, local copies, waits for them, and re-layouts  1.32 us

profile of v6, /device:TPU:1, one launch (start us, length us, event | category | flops | bytes accessed | tf_op | source)
XLA Modules:
  0.0 53.6 jit_solution(10017415235020257291)
XLA Ops:
  0.0 52.3 %shard_map.73 = f32[16,2,128,128]{3,2,1,0:T(8,128)S(1)} custom-call(f32[16,2,128,128]{3,2,1,0:T(8,128)} %bitcast.9, f32[16,2,128,128]{3,2,1,0:T(8,128)} %bitcast.10, f32[16,2,128,128]{3,2,1,0:T(8,128)} %bitcast.11, s32[128,128]{1,0:T(8,128)} %bitcast.12, f32[128,128]{1,0:T(8,128)} %bitcast.13, bf16[4,16,128,192]{3,2,1,0:T(8,128)(2,1)} %constant.4.clone.ahead_hbm, ...), custom_call_target="tpu_custom_call" | custom-call | flops 10000000000 | bytes 20000000 | tf_op jit(solution)/shard_map/pallas_call | solution.py:485
  52.3 1.3 %copy.10 = f32[16,2,1,128,128]{4,3,2,1,0:T(8,128)} copy(f32[16,2,1,128,128]{4,3,2,1,0:T(8,128)S(1)} %bitcast.8) | data formatting | bytes 4194304
